TPU v7x, 256 devices: a whole 4x4x8 slice. The times are simulated.
256 devices in a mesh: panel: 2 (over x_hi), lat: 8 (over z), lon: 16 (over x_lo, y, core).
Axes of the slice: x: 4 (x_hi: 2, x_lo: 2; x = x_hi * 2 + x_lo), y: 4, z: 8, core: 2. Of those that a mesh axis runs over, the one named last changes fastest.
Arguments:
- state: float32 [2, 128, 256, 8, 128], P('panel', 'lat', 'lon'), may hold values from -6 to 6
- rim_base: int32 [2, 1536, 2], P('panel', ('lat', 'lon')), may hold values from 1 to 253, as said below
- rim_weight: float32 [2, 1536, 16], P('panel', ('lat', 'lon')), may hold values from -0.1 to 0.2
- rim_angle: float32 [2, 1536], P('panel', ('lat', 'lon')), may hold values from -3 to 3
- rim_target: int32 [2, 1536, 2], P('panel'), may hold values from -2 to 257, as said below
Outputs:
- change: float32 [2, 128, 256, 8, 128], P('panel', 'lat', 'lon')
Inputs may be any that keep to these rules, and one draw needn't show every extreme that they name: `rim_base`: entry e of panel p names a base cell (row, column) of panel p whose 4 x 4 donor stencil, rows and columns from base - 1 to base + 2, lies inside the panel; the base cell lies in block e // 12 of 16 x 16 cells, blocks numbered row by row with 16 blocks to a row. `rim_target`: the rim of panel q is a loop of 1536 positions: rows -2 and -1 at columns 0 to 256 - 1 (column by column, row -2 first), then columns 256 and 257 at rows 0 to 128 - 1 (row by row), then rows 128 and 129 at columns 255 down to 0, then columns -2 and -1 at rows 127 down to 0. Entry e, with b = e // 12 and i = e % 12, fills loop position (i * 128 + b + o_q) mod 1536, for one offset o_q per panel.
All inputs are finite; a program needn't handle non-finite values.
Results may differ from a plain program's by a relative error of at most 0.00015.
Values sent between devices are 32-bit elements; how exact they have to be, the bound alone decides.
A program may use at most 64 MiB of HBM per device.

v0:
```python
import math

import jax
import jax.numpy as jnp
import numpy as np
from jax import lax
from jax.experimental import pallas as pl
from jax.experimental.pallas import tpu as pltpu
from jax.sharding import PartitionSpec as P

NTH, NPH, NR, NF, CB = 128, 256, 128, 8, 16
LAT, LON = NTH // CB, NPH // CB
LOOP = 1536
ENTRIES = 12
ETA = np.float32(0.2)
NU = np.float32(0.2)
KAPPA = np.float32(0.3)
LIFT = np.float32(0.5)
DT = np.float32(0.2)
MESH = pl.DeviceIdType.MESH

DTHETA = math.pi / (2 * NTH)
DPHI = 1.5 * math.pi / NPH
H_THETA = np.float32(0.5 / DTHETA)


def row_table():
    g = np.arange(-4, NTH + 4)
    sine = lambda k: np.sin(math.pi / 4 + (k + 0.5) * DTHETA)
    s = sine(g)
    half = 0.5 / DTHETA
    return np.stack([sine(g + 1) * half / s, sine(g - 1) * half / s, 0.5 / DPHI / s]).astype(
        np.float32
    )


def level_table():
    scale = 2.0 * NTH / math.pi
    dr = 0.65 * scale / NR
    r = 0.35 * scale + (np.arange(NR) + 0.5) * dr
    half = 0.5 / dr
    up = np.where(np.arange(NR) < NR - 1, half, 0.0)
    down = np.where(np.arange(NR) > 0, half, 0.0)
    r_up, r_down = np.roll(r, -1), np.roll(r, 1)
    rows = [
        1 / r,
        up * r_up / r,
        down * r_down / r,
        up,
        down,
        up * r_up**2 / r**2,
        down * r_down**2 / r**2,
        0 * r,
    ]
    return np.stack(rows).astype(np.float32)


def above(x):
    return pltpu.roll(x, NR - 1, 1)


def below(x):
    return pltpu.roll(x, 1, 1)


def cross(a, b):
    return (
        a[1] * b[2] - a[2] * b[1],
        a[2] * b[0] - a[0] * b[2],
        a[0] * b[1] - a[1] * b[0],
    )


def kernel(
    rows, levels, state, base_hbm, weight_hbm, angle_hbm, target_hbm,
    out,
    Y0, Y1, K1, L1, V,
    R00, R01, R10, R11, Q, W00, W01, W10, W11, X00, X01, X10, X11,
    ZH, ZV, LZ, trig, far, base, weight, angle, near_at, far_at, rows_s, levels_s, slopes, O,
    halo_send, halo_recv, a_send, a_recv, b_send, b_recv, x_send, x_recv, part_send, part_recv, wide_send, wide_recv, misc, heard,
):
    p, a, c = lax.axis_index("panel"), lax.axis_index("lat"), lax.axis_index("lon")
    b = a * LON + c
    Y = (Y0, Y1)
    R = ((R00, R01), (R10, R11))
    W = ((W00, W01), (W10, W11))
    X = ((X00, X01), (X10, X11))

    steps = [(1, 0), (-1, 0), (1, 1), (1, -1), (-1, 1), (-1, -1), (0, 1), (0, -1)]

    def span(step):
        if step == 0:
            return 0, 2, CB
        return (CB - 2, 0, 2) if step > 0 else (0, CB + 2, 2)

    def halo_copy(e, k, part=None):
        dr, dc = steps[k]
        r0, rd, rn = span(dr)
        c0, cd, cn = span(dc)
        if part is not None:
            first, count = ((0, 2), (2, CB - 4), (CB - 2, 2))[part]
            if dr:
                c0, cd, cn = c0 + first, cd + first, count
            else:
                r0, rd, rn = r0 + first, rd + first, count
        if e == 0:
            src = state.at[pl.ds(r0, rn), pl.ds(c0, cn)]
        else:
            src = Y[1].at[pl.ds(r0 + 2, rn), pl.ds(c0 + 2, cn)]
        return pltpu.make_async_remote_copy(
            src_ref=src,
            dst_ref=Y[e].at[pl.ds(rd, rn), pl.ds(cd, cn)],
            send_sem=halo_send.at[e, k] if part is None else part_send.at[k, part],
            recv_sem=halo_recv.at[e, k] if part is None else part_recv.at[k, part],
            device_id=(p, a + dr, c + dc),
            device_id_type=MESH,
        )

    def exists(dr, dc):
        ok = None
        for pos, d, n in ((a, dr, LAT), (c, dc, LON)):
            if d:
                t = (pos < n - 1) if d > 0 else (pos > 0)
                ok = t if ok is None else jnp.logical_and(ok, t)
        return ok

    def halo_start(e):
        for k, (dr, dc) in enumerate(steps):
            @pl.when(exists(dr, dc))
            def _():
                halo_copy(e, k).start()

    def halo_wait_recv(e):
        for k, (dr, dc) in enumerate(steps):
            @pl.when(exists(-dr, -dc))
            def _():
                halo_copy(e, k).wait_recv()

    def halo_wait_send(e):
        for k, (dr, dc) in enumerate(steps):
            @pl.when(exists(dr, dc))
            def _():
                halo_copy(e, k).wait_send()

    def rim_part(dr, dc, part):
        if part == 1:
            return jnp.bool_(False)
        if dc:
            return on_top if part == 0 else on_bottom
        return on_left if part == 0 else on_right

    def second_halo(sending, act):
        for k, (dr, dc) in enumerate(steps):
            there = exists(dr, dc) if sending else exists(-dr, -dc)
            if dr and dc:
                @pl.when(there)
                def _():
                    act(halo_copy(1, k))
                continue
            for part in range(3):
                @pl.when(jnp.logical_and(there, jnp.logical_not(rim_part(dr, dc, part))))
                def _():
                    act(halo_copy(1, k, part))

    on_top, on_bottom = a == 0, a == LAT - 1
    on_right, on_left = c == LON - 1, c == 0
    active = (jnp.logical_or(on_top, on_bottom), jnp.logical_or(on_right, on_left))
    at_right = c >= LON // 2
    sign = (jnp.where(on_top, 1, -1), jnp.where(at_right, 1, -1))
    rank = (jnp.where(on_top, c, LON - 1 - c), jnp.where(at_right, a, LAT - 1 - a))
    groups = (LON // 4, LAT // 4)
    segment = tuple(lax.rem(u, 4) for u in rank)
    has_next = tuple(u // 4 < n - 1 for u, n in zip(rank, groups))
    has_prev = tuple(u // 4 > 0 for u in rank)
    relays = (active[0], jnp.logical_or(c < 2, c >= LON - 2))
    member = (
        lax.rem(c, 4) ^ 2,
        2 * lax.rem(segment[1], 2) + lax.rem(c, 2),
    )
    own_slot = member
    to_next = (has_next[0], jnp.logical_and(has_next[1], segment[1] >= 2))
    to_prev = (has_prev[0], jnp.logical_and(has_prev[1], segment[1] < 2))

    def along(side, step):
        if side == 0:
            return (p, a, c + sign[0] * step)
        return (p, a + sign[1] * step, jnp.where(at_right, LON - 1, 0))

    def wide_copy(side, way):
        first = (jnp.where(on_top, 0, CB - 4), jnp.where(on_left, 0, CB - 4))[side]
        lands = (jnp.where(on_top, 2, 0), jnp.where(on_left, 2, 0))[side]
        near, far_end = (CB - 4, 0) if way > 0 else (2, CB + 6)
        if side == 0:
            src = state.at[pl.ds(first, 4), pl.ds(near, 2)]
            dst = ZH.at[pl.ds(lands, 4), pl.ds(far_end, 2)]
            dev = (p, a, c + way)
        else:
            src = state.at[pl.ds(near, 2), pl.ds(first, 4)]
            dst = ZV.at[pl.ds(far_end, 2), pl.ds(lands, 4)]
            dev = (p, a + way, c)
        k = 0 if way > 0 else 1
        return pltpu.make_async_remote_copy(
            src_ref=src, dst_ref=dst, send_sem=wide_send.at[side, k],
            recv_sem=wide_recv.at[side, k], device_id=dev, device_id_type=MESH,
        )

    def wide(side, sending, act):
        for way in (1, -1):
            step = way if sending else -way
            there = exists(0, step) if side == 0 else exists(step, 0)

            @pl.when(there)
            def _():
                act(wide_copy(side, way))

    m_src = lax.rem(c, 4)

    def a_copy(e, g, again=0):
        half, core = m_src // 2, lax.rem(m_src, 2)
        if g < 4:
            side, dev = 0, (1 - p, 0, 4 * g + (m_src ^ 2))
        elif g < 6:
            side, dev = 1, (1 - p, 4 * (g - 4) + 2 * again + half, LON - 2 + core)
        elif g < 10:
            side, dev = 0, (1 - p, LAT - 1, 4 * (9 - g) + (m_src ^ 2))
        else:
            side, dev = 1, (1 - p, LAT - 1 - (4 * (g - 10) + 2 * again + half), core)
        return pltpu.make_async_remote_copy(
            src_ref=V.at[e, g],
            dst_ref=R[e][side].at[4 * a + c // 4],
            send_sem=a_send.at[e, again],
            recv_sem=a_recv.at[e, side],
            device_id=dev,
            device_id_type=MESH,
        )

    column_groups = (4, 5, 10, 11)

    def a_wait_send(e):
        for again, count in ((0, ENTRIES), (1, 4)):
            pltpu.make_async_remote_copy(
                src_ref=V.at[e, pl.ds(0, count)],
                dst_ref=R[e][0].at[pl.ds(0, count)],
                send_sem=a_send.at[e, again],
                recv_sem=a_recv.at[e, 0],
                device_id=(1 - p, a, c),
                device_id_type=MESH,
            ).wait_send()

    def a_wait_recv(e, side):
        pltpu.make_async_remote_copy(
            src_ref=R[e][side],
            dst_ref=R[e][side],
            send_sem=a_send.at[e, 0],
            recv_sem=a_recv.at[e, side],
            device_id=(1 - p, a, c),
            device_id_type=MESH,
        ).wait_recv()

    def b_copy(e, side, s, slot, k):
        first, count = (0, 12) if e == 0 else (1, 10)
        return pltpu.make_async_remote_copy(
            src_ref=Q.at[e, side, pl.ds(8 * s + first, count)],
            dst_ref=W[e][side].at[slot, pl.ds(first, count)],
            send_sem=b_send.at[e, side, k],
            recv_sem=b_recv.at[e, side, slot],
            device_id=along(side, s - segment[side]),
            device_id_type=MESH,
        )

    def x_copy(e, side, way):
        return pltpu.make_async_remote_copy(
            src_ref=Q.at[e, side, pl.ds(32 + e if way == 0 else 2, 2 - e)],
            dst_ref=X[e][side].at[way, member[side], pl.ds(e if way == 0 else 0, 2 - e)],
            send_sem=x_send.at[e, side, way],
            recv_sem=x_recv.at[e, side, way],
            device_id=along(side, (4 if way == 0 else -1) - segment[side]),
            device_id_type=MESH,
        )

    def x_wait_recv(e, side, way):
        pltpu.make_async_remote_copy(
            src_ref=X[e][side].at[way, :, pl.ds(e if way == 0 else 0, 2 - e)],
            dst_ref=X[e][side].at[way, :, pl.ds(e if way == 0 else 0, 2 - e)],
            send_sem=x_send.at[e, side, way],
            recv_sem=x_recv.at[e, side, way],
            device_id=along(side, 1),
            device_id_type=MESH,
        ).wait_recv()

    def greet():
        barrier = pltpu.get_barrier_semaphore()

        def hello(dev):
            pl.semaphore_signal(barrier, inc=1, device_id=dev, device_id_type=MESH)

        @pl.loop(0, LON)
        def _(k):
            hello((1 - p, a, k))

        @pl.loop(1, LAT)
        def _(k):
            hello((p, lax.rem(a + k, LAT), c))

        @pl.when(active[0])
        def _():
            @pl.loop(1, LON)
            def _(k):
                hello((p, a, lax.rem(c + k, LON)))

        awaited = jnp.where(active[0], LON + LAT - 1 + LON - 1, LON + LAT - 1)
        for dr, dc in steps:
            if not dc:
                continue
            there = exists(dr, dc)
            awaited += there.astype(jnp.int32)

            @pl.when(there)
            def _():
                hello((p, a + dr, c + dc))

        return lambda: pl.semaphore_wait(barrier, awaited)

    def pass_on():
        @pl.loop(1, LAT)
        def _(k):
            pl.semaphore_signal(
                heard, inc=1, device_id=(p, lax.rem(a + k, LAT), c), device_id_type=MESH
            )

    def flat(e):
        return Y[e].reshape(21 * 20 * NF, NR)

    def interpolate(e, o_far):
        turn = (b + o_far) >> 7
        sub = lax.broadcasted_iota(jnp.int32, (NF, NR), 0)
        first = jnp.logical_or(sub == 1, sub == 4)
        second = jnp.logical_or(sub == 2, sub == 5)
        turned = jnp.logical_or(first, second)

        for g in (*column_groups, 0, 3, 6, 9, 1, 2, 7, 8):
            i = lax.rem(g - turn + 2 * ENTRIES, ENTRIES)
            r0 = jnp.clip(base[0, i] - a * CB + 1, 1, CB)
            c0 = jnp.clip(base[1, i] - c * CB + 1, 1, CB)
            parts = []
            for x in range(4):
                acc = None
                for y in range(4):
                    term = weight[i, 0, 4 * x + y] * Y[e][r0 + x, c0 + y]
                    acc = term if acc is None else acc + term
                parts.append(acc)
            m = (parts[0] + parts[1]) + (parts[2] + parts[3])
            cosine = trig[0, pl.ds(i, 1), :]
            sine = trig[1, pl.ds(i, 1), :]
            partner = jnp.where(first, -pltpu.roll(m, NF - 1, 0), pltpu.roll(m, 1, 0))
            V[e, g] = jnp.where(turned, cosine * m + sine * partner, m)
            for again in range(2 if g in column_groups else 1):
                a_copy(e, g, again).start()

    def is_self(side, s):
        here = segment[side] == s
        return here if side == 0 else jnp.logical_and(here, active[1])

    def side_loop(fn, roles):
        for side in range(2):
            @pl.when(roles[side])
            def _():
                fn(side)

    def spread(e, side, o_near):
        shift = (member[side] + o_near) >> 2
        for n in range(36):
            Q[e, side, n] = R[e][side][(n - 2 - shift + LOOP) & 31]
        for way, has in ((0, to_next), (1, to_prev)):
            @pl.when(has[side])
            def _():
                x_copy(e, side, way).start()
        for k in ((2, 3, 1, 0), (1, 0))[side]:
            s = segment[side] ^ k

            @pl.when(jnp.logical_not(is_self(side, s)))
            def _():
                b_copy(e, side, s, member[side], k).start()

        @pl.when(active[side])
        def _():
            for n in range(12):
                W[e][side][member[side], n] = Q[e, side, 8 * segment[side] + n]

    def spread_wait_send(e, side):
        for k in range((4, 2)[side]):
            s = segment[side] ^ k

            @pl.when(jnp.logical_not(is_self(side, s)))
            def _():
                b_copy(e, side, s, member[side], k).wait_send()
        for way, has in ((0, to_next), (1, to_prev)):
            @pl.when(has[side])
            def _():
                x_copy(e, side, way).wait_send()

    def collect(e, side, o_near):
        for s in range(4):
            @pl.when(own_slot[side] != s)
            def _():
                b_copy(e, side, 0, s, 0).wait_recv()
        for way, has, edge in ((0, has_prev, 0), (1, has_next, 3)):
            @pl.when(jnp.logical_and(has[side], segment[side] == edge))
            def _():
                x_wait_recv(e, side, way)

        def place(cell, far_cell):
            for rho in range(4):
                who = (rho - o_near + LOOP) & 3
                for n in range(0 if e == 0 else 1, 12 if e == 0 else 11):
                    value = W[e][side][who, n]
                    if n < 2 or n > 9:
                        way, has, edge = (0, has_prev, 0) if n < 2 else (1, has_next, 3)
                        far_value = jnp.where(has[side], X[e][side][way, who, n if n < 2 else n - 10], 0.0)
                        value = jnp.where(segment[side] == edge, far_value, value)
                    h, o = 2 * n + rho // 2, rho % 2
                    if 1 <= n <= 10:
                        r, q = cell(h - 2, o)
                        Y[e][r, q] = value
                    else:
                        r, q = far_cell(h, o)
                        (ZH, ZV)[side][r, q] = value

        cells = (
            (
                (on_top, lambda h, o: (o, h), lambda h, o: (o, h)),
                (on_bottom, lambda h, o: (18 + o, 19 - h), lambda h, o: (4 + o, 23 - h)),
            ),
            (
                (on_right, lambda h, o: (h, 18 + o), lambda h, o: (h, 4 + o)),
                (on_left, lambda h, o: (19 - h, o), lambda h, o: (23 - h, o)),
            ),
        )[side]
        for on, cell, far_cell in cells:
            @pl.when(on)
            def _():
                place(cell, far_cell)

    def curl(A, ap, am, bb, br, rh):
        a1, a2 = A(1, 0, 0), A(2, 0, 0)
        return (
            ri * ((A(2, 1, 0) * ap - A(2, -1, 0) * am) - (A(1, 0, 1) - A(1, 0, -1)) * bb),
            (A(0, 0, 1) - A(0, 0, -1)) * br - (above(a2) * cp - below(a2) * cm),
            (above(a1) * cp - below(a1) * cm) - (A(0, 1, 0) - A(0, -1, 0)) * rh,
        )

    def first_values(ld, ap, am, bb, br):
        u = [ld(k, 0, 0) for k in range(3)]
        mag = [ld(3 + k, 0, 0) for k in range(3)]
        w = curl(lambda k, dg, dj: ld(k, dg, dj), ap, am, bb, br, rh)
        cur = curl(lambda k, dg, dj: ld(3 + k, dg, dj), ap, am, bb, br, rh)
        ind = cross(u, mag)
        el = [ind[k] - ETA * cur[k] for k in range(3)]
        t = ld(6, 0, 0)
        grad = [
            above(t) * dp - below(t) * dm,
            (ld(6, 1, 0) - ld(6, -1, 0)) * rh,
            (ld(6, 0, 1) - ld(6, 0, -1)) * br,
        ]
        head = ld(7, 0, 0) + np.float32(0.5) * (u[0] * u[0] + u[1] * u[1] + u[2] * u[2])
        return [*w, *cur, *el, *grad, head]

    def second_values(ld, mid, ap, am, bb, br):
        Wv, J, E, T, H = (lambda k, dg, dj, q=q: mid(q + k, dg, dj) for q in (0, 3, 6, 9, 12))
        cw = curl(Wv, ap, am, bb, br, rh)
        ce = curl(E, ap, am, bb, br, rh)
        u = [ld(k, 0, 0) for k in range(3)]
        mag = [ld(3 + k, 0, 0) for k in range(3)]
        w = [Wv(k, 0, 0) for k in range(3)]
        cur = [J(k, 0, 0) for k in range(3)]
        adv, lor = cross(u, w), cross(cur, mag)
        h = H(0, 0, 0)
        slope = (
            above(h) * dp - below(h) * dm,
            (H(0, 1, 0) - H(0, -1, 0)) * rh,
            (H(0, 0, 1) - H(0, 0, -1)) * br,
        )
        t0 = T(0, 0, 0)
        lap = (above(t0) * ep - below(t0) * em) + ri * (
            (T(1, 1, 0) * ap - T(1, -1, 0) * am) + (T(2, 0, 1) - T(2, 0, -1)) * bb
        )
        div = (above(u[0]) * ep - below(u[0]) * em) + ri * (
            (ld(1, 1, 0) * ap - ld(1, -1, 0) * am) + (ld(2, 0, 1) - ld(2, 0, -1)) * bb
        )
        ru = [adv[k] + lor[k] - slope[k] - NU * cw[k] for k in range(3)]
        ru[0] = ru[0] + LIFT * ld(6, 0, 0)
        rt = KAPPA * lap - (u[0] * t0 + u[1] * T(1, 0, 0) + u[2] * T(2, 0, 0))
        return [*ru, *ce, rt, -div]

    def eight(first, step):
        return pl.ds(first, 8) if step == 1 else pl.ds(first, 8, stride=step)

    def factors(i, column):
        if column:
            ap, am, bb = (slopes[k, pl.ds(i + 3, 8), :] for k in range(3))
        else:
            ap, am, bb = (rows_s[k, a * CB + i + 4] for k in range(3))
        return ap, am, bb, ri * bb

    def block_view(e):
        return (
            flat(e), 20, lambda i, j: (i + 2) * 20 + j + 2,
            L1, 24, lambda q, i, j: (q * 18 + i + 1) * 24 + j + 1,
        )

    def row_view(r0):
        return (
            ZH.reshape(6 * 24 * NF, NR), 24, lambda i, j: (i - r0) * 24 + j + 4,
            LZ, 24, lambda q, i, j: (q * 4 + i - r0 - 1) * 24 + j + 3,
        )

    def column_view(c0):
        return (
            ZV.reshape(25 * 6 * NF, NR), 6, lambda i, j: (i + 4) * 6 + j - c0,
            LZ, 4, lambda q, i, j: (q * 24 + i + 3) * 4 + j - c0 - 1,
        )

    def loader(view, i, j, column):
        cells, width, cell = view[:3]
        step = width * NF if column else NF
        return lambda f, dg, dj: cells[eight(cell(i + dg, j + dj) * NF + f, step), :]

    def first_pass(view, i, j, column=False):
        store, width, place = view[3:]
        values = first_values(loader(view, i, j, column), *factors(i, column))
        for q, v in enumerate(values):
            store[eight(place(q, i, j), width if column else 1), :] = v

    def second_pass(e, view, i, j, column=False):
        store, width, place = view[3:]

        def mid(q, dg, dj):
            return store[eight(place(q, i + dg, j + dj), width if column else 1), :]

        sink = keep if e == 0 else finish
        values = second_values(loader(view, i, j, column), mid, *factors(i, column))
        for f, v in enumerate(values):
            sink(i, j, f, v, column)

    def whole(e):
        view = block_view(e)

        @pl.loop(0, 18)
        def _(n):
            for j in (-1, 7, 9):
                first_pass(view, n - 1, j)

        @pl.loop(0, 16)
        def _(i):
            for j in (0, 8):
                second_pass(e, view, i, j)

    row_edge = jnp.where(on_top, -2, CB - 4)
    column_edge = jnp.where(on_left, -2, CB - 4)

    def wide_strips():
        @pl.when(active[0])
        def _():
            wide(0, False, lambda copy: copy.wait_recv())
            ZH[:, pl.ds(2, 20)] = Y0[pl.ds(row_edge + 2, 6)]
            view = row_view(row_edge)
            for n in range(4):
                for j in (-3, 5, 11):
                    first_pass(view, row_edge + 1 + n, j)
            for n in range(2):
                for j in (-2, 6, 10):
                    second_pass(0, view, row_edge + 2 + n, j)

        @pl.when(active[1])
        def _():
            wide(1, False, lambda copy: copy.wait_recv())
            ZV[pl.ds(2, 20)] = Y0[pl.ds(0, 20), pl.ds(column_edge + 2, 6)]
            view = column_view(column_edge)
            for n in range(4):
                for i in (-3, 5, 11):
                    first_pass(view, i, column_edge + 1 + n, True)
            for n in range(2):
                for i in (-2, 6, 10):
                    second_pass(0, view, i, column_edge + 2 + n, True)

    def strips():
        view = block_view(1)

        @pl.when(active[0])
        def _():
            first = jnp.where(on_top, -1, CB - 1)
            for n in range(2):
                for j in (-1, 7, 9):
                    first_pass(view, first + n, j)

        @pl.when(active[1])
        def _():
            first = jnp.where(on_left, -1, CB - 1)
            for n in range(2):
                for i in (-1, 7, 9):
                    first_pass(view, i, first + n, True)

        @pl.when(active[0])
        def _():
            for n in range(2):
                for j in (0, 8):
                    second_pass(1, view, row_edge + 2 + n, j)

        @pl.when(active[1])
        def _():
            for n in range(2):
                for i in (0, 8):
                    second_pass(1, view, i, column_edge + 2 + n, True)

    y_second = flat(1)
    y_first = flat(0)
    out_flat = O.reshape((CB + 1) * CB * NF, NR)

    def keep(i, j, f, v, column):
        K1[eight((f * 20 + i + 2) * 24 + j + 4, 24 if column else 1), :] = v
        at = eight(((i + 2) * 20 + j + 2) * NF + f, 20 * NF if column else NF)
        y_second[at, :] = y_first[at, :] + DT * v

    def finish(i, j, f, v, column):
        k1 = K1[eight((f * 20 + i + 2) * 24 + j + 4, 24 if column else 1), :]
        at = eight((i * CB + j) * NF + f, CB * NF if column else NF)
        out_flat[at, :] = np.float32(0.1) * (k1 + v)

    def fetch(k, src, dst):
        copy = pltpu.make_async_copy(src, dst, misc.at[k])
        copy.start()
        return copy

    inner, two = CB - 4, CB - 2
    parts = (
        (2, inner, 2, inner, None),
        (0, 2, 0, CB, jnp.logical_or(on_top, active[1])),
        (two, 2, 0, CB, jnp.logical_or(on_bottom, active[1])),
        (2, inner, 0, 2, on_left),
        (2, inner, two, 2, on_right),
    )

    def store_copy(k):
        r0, rn, c0, cn, _ = parts[k]
        at = (pl.ds(r0, rn), pl.ds(c0, cn))
        return pltpu.make_async_copy(O.at[at], out.at[at], misc.at[10 + k])

    def store(early):
        for k, (*_, reached) in enumerate(parts):
            if reached is None:
                if early:
                    store_copy(k).start()
                continue

            @pl.when(jnp.logical_not(reached) if early else reached)
            def _():
                store_copy(k).start()

    hear = greet()
    corner = target_hbm.at[:, pl.ds(0, 128)]
    local = fetch(0, state, Y0.at[pl.ds(2, CB), pl.ds(2, CB)])
    small = [
        fetch(3, angle_hbm, angle),
        fetch(4, corner, near_at),
        fetch(5, base_hbm, base),
        fetch(6, weight_hbm, weight),
        fetch(7, rows, rows_s),
        fetch(9, levels, levels_s),
    ]
    hear()
    halo_start(0)
    pass_on()
    tell = pltpu.make_async_remote_copy(
        src_ref=corner, dst_ref=far, send_sem=misc.at[1], recv_sem=misc.at[2],
        device_id=(1 - p, a, c), device_id_type=MESH,
    )
    tell.start()
    side_loop(lambda side: wide(side, True, lambda copy: copy.start()), active)

    for copy in small:
        copy.wait()
    ri = levels_s[0:1, :]
    cp, cm = levels_s[1:2, :], levels_s[2:3, :]
    dp, dm = levels_s[3:4, :], levels_s[4:5, :]
    ep, em = levels_s[5:6, :], levels_s[6:7, :]
    rh = ri * H_THETA
    trig[0] = jnp.zeros((16, NR), jnp.float32)
    for i in range(ENTRIES):
        trig[0, i : i + 1, :] = jnp.full((1, NR), angle[0, i], jnp.float32)
    turned = trig[0]
    trig[0] = jnp.cos(turned)
    trig[1] = jnp.sin(turned)

    for i in range(24):
        gi = jnp.minimum(a * CB + i + 1, NTH + 7)
        for k in range(3):
            slopes[k, i : i + 1, :] = jnp.full((1, NR), rows_s[k, gi], jnp.float32)

    tell.wait_recv()
    fetch(8, far, far_at).wait()
    local.wait()
    o_near = loop_place(near_at[0, 0], near_at[1, 0])
    o_far = loop_place(far_at[0, 0], far_at[1, 0])

    for e in range(2):
        if e == 0:
            halo_wait_recv(0)
        else:
            second_halo(False, lambda copy: copy.wait_recv())
        if e == 0:
            pl.semaphore_wait(heard, LAT - 1)
        interpolate(e, o_far)
        whole(e)
        if e == 0:
            second_halo(True, lambda copy: copy.start())
        else:
            store(early=True)

        def middle(side):
            a_wait_recv(e, side)
            spread(e, side, o_near)

        side_loop(middle, relays)
        side_loop(lambda side: collect(e, side, o_near), active)
        if e == 0:
            wide_strips()
        else:
            strips()
            store(early=False)

    tell.wait_send()
    for k in range(len(parts)):
        store_copy(k).wait()
    for e in range(2):
        if e == 0:
            halo_wait_send(0)
            side_loop(lambda side: wide(side, True, lambda copy: copy.wait_send()), active)
        else:
            second_halo(True, lambda copy: copy.wait_send())
        a_wait_send(e)
        side_loop(lambda side: spread_wait_send(e, side), relays)


def loop_place(row, col):
    return jnp.where(
        row < 0,
        2 * col + row + 2,
        jnp.where(
            col >= NPH,
            2 * NPH + 2 * row + col - NPH,
            jnp.where(
                row >= NTH,
                2 * NPH + 2 * NTH + 2 * (NPH - 1 - col) + row - NTH,
                4 * NPH + 2 * NTH + 2 * (NTH - 1 - row) + col + 2,
            ),
        ),
    )


def per_device(state, rim_base, rim_weight, rim_angle, rim_target):
    anywhere = pl.BlockSpec(memory_space=pl.ANY)
    f32 = jnp.float32
    result = pl.pallas_call(
        kernel,
        out_shape=jax.ShapeDtypeStruct((CB, CB, NF, NR), f32),
        in_specs=[anywhere] * 7,
        out_specs=anywhere,
        scratch_shapes=[
            pltpu.VMEM((21, 20, NF, NR), f32),
            pltpu.VMEM((21, 20, NF, NR), f32),
            pltpu.VMEM((NF * 20 * 24 + 48, NR), f32),
            pltpu.VMEM((13 * 18 * 24 + 48, NR), f32),
            pltpu.VMEM((2, ENTRIES, NF, NR), f32),
            *[pltpu.VMEM((32, NF, NR), f32)] * 4,
            pltpu.VMEM((2, 2, 36, NF, NR), f32),
            *[pltpu.VMEM((4, 12, NF, NR), f32)] * 4,
            *[pltpu.VMEM((2, 4, 2, NF, NR), f32)] * 4,
            pltpu.VMEM((6, 24, NF, NR), f32),
            pltpu.VMEM((25, 6, NF, NR), f32),
            pltpu.VMEM((13 * 96 + 8, NR), f32),
            pltpu.VMEM((2, 16, NR), f32),
            pltpu.VMEM((2, 128), jnp.int32),
            pltpu.SMEM((2, ENTRIES), jnp.int32),
            pltpu.SMEM((ENTRIES, 1, 16), f32),
            pltpu.SMEM((1, ENTRIES), f32),
            pltpu.SMEM((2, 128), jnp.int32),
            pltpu.SMEM((2, 128), jnp.int32),
            pltpu.SMEM((3, NTH + 8), f32),
            pltpu.VMEM((8, NR), f32),
            pltpu.VMEM((3, 24, NR), f32),
            pltpu.VMEM((CB + 1, CB, NF, NR), f32),
            pltpu.SemaphoreType.DMA((2, 8)),
            pltpu.SemaphoreType.DMA((2, 8)),
            pltpu.SemaphoreType.DMA((2, 2)),
            pltpu.SemaphoreType.DMA((2, 2)),
            pltpu.SemaphoreType.DMA((2, 2, 4)),
            pltpu.SemaphoreType.DMA((2, 2, 4)),
            pltpu.SemaphoreType.DMA((2, 2, 2)),
            pltpu.SemaphoreType.DMA((2, 2, 2)),
            pltpu.SemaphoreType.DMA((8, 3)),
            pltpu.SemaphoreType.DMA((8, 3)),
            pltpu.SemaphoreType.DMA((2, 2)),
            pltpu.SemaphoreType.DMA((2, 2)),
            pltpu.SemaphoreType.DMA((15,)),
            pltpu.SemaphoreType.REGULAR,
        ],
        compiler_params=pltpu.CompilerParams(
            collective_id=0, has_side_effects=True, vmem_limit_bytes=56 << 20
        ),
    )(
        jnp.asarray(row_table()),
        jnp.asarray(level_table()),
        state[0],
        rim_base[0].T,
        jnp.transpose(rim_weight, (1, 0, 2)),
        rim_angle,
        rim_target[0].T,
    )
    return result[None]


def solution(mesh):
    return jax.shard_map(
        per_device,
        mesh=mesh,
        in_specs=(
            P("panel", "lat", "lon", None, None),
            P("panel", ("lat", "lon"), None),
            P("panel", ("lat", "lon"), None),
            P("panel", ("lat", "lon")),
            P("panel", None, None),
        ),
        out_specs=P("panel", "lat", "lon", None, None),
        check_vma=False,
    )
```

profile of v0, /device:TPU:1, one launch (start us, length us, event | category | flops | bytes accessed | tf_op | source)
XLA Modules:
  0.0 42.9 jit_solution(280416957842380594)
XLA Ops:
  0.0 40.6 %shard_map.73 = f32[16,16,8,128]{3,2,1,0:T(8,128)} custom-call(f32[3,136]{1,0:T(4,128)} %constant.4.clone.rows, f32[8,128]{1,0:T(8,128)} %constant.5.clone.levels, f32[16,16,8,128]{3,2,1,0:T(8,128)} %bitcast.10, s32[2,12]{1,0:T(2,128)} %bitcast.13, f32[12,1,16]{2,1,0:T(1,128)} %bitcast.12, f32[1,12]{1,0:T(1,128)} %angle_hbm.1, s32[2,1536]{1,0:T(2,128)} %bitcast.11), custom_call_target="tpu_custom_call" | custom-call | tf_op jit(solution)/shard_map/pallas_call | solution.py:763
  40.6 2.3 %copy.9 = f32[1,16,16,8,128]{4,3,2,1,0:T(8,128)} copy(f32[1,16,16,8,128]{4,3,2,1,0:T(8,128)} %bitcast.9) | data formatting | bytes 2097152
where the time goes:
time: 43 us; the launch traced here: 42.9 us
  Pallas kernels  40.6 us (94%)
  local copies, waits for them, and re-layouts  2.3 us (5%)
    pallas_call x1, Pallas kernels, per_device(): pl.pallas_call(kernel, out_shape=jax.ShapeDtypeStruct((CB, CB, NF, NR), f...  40.6 us
    unnamed x1, local copies, waits for them, and re-layouts  2.3 us

commit v1 on v0

--- a/solution.py
+++ b/solution.py
@@ -369,13 +369,18 @@
 
     def spread(e, side, o_near):
         shift = (member[side] + o_near) >> 2
-        for n in range(36):
-            Q[e, side, n] = R[e][side][(n - 2 - shift + LOOP) & 31]
+        def turn(slots):
+            for n in slots:
+                Q[e, side, n] = R[e][side][(n - 2 - shift + LOOP) & 31]
+
+        ends = (2, 3, 32, 33)
+        turn(ends)
         for way, has in ((0, to_next), (1, to_prev)):
             @pl.when(has[side])
             def _():
                 x_copy(e, side, way).start()
-        for k in ((2, 3, 1, 0), (1, 0))[side]:
+        turn([n for n in range(36) if n not in ends])
+        for k in ((3, 2, 1, 0), (1, 0))[side]:
             s = segment[side] ^ k
 
             @pl.when(jnp.logical_not(is_self(side, s)))

time: 43 us -> 42.5 us (0.988)
  Pallas kernels: 40.6 us -> 39.9 us
    pallas_call x1, Pallas kernels: 40.6 us -> 39.9 us  [per_device(): pl.pallas_call(kernel, out_shape=jax.ShapeDtypeStruct((CB, CB, NF, NR), f...]
where the time goes in v1:
time: 42.5 us; the launch traced here: 42.2 us
  Pallas kernels  39.9 us (94%)
  local copies, waits for them, and re-layouts  2.3 us (5%)
    pallas_call x1, Pallas kernels, per_device(): pl.pallas_call(kernel, out_shape=jax.ShapeDtypeStruct((CB, CB, NF, NR), f...  39.9 us
    unnamed x1, local copies, waits for them, and re-layouts  2.3 us

profile of v1, /device:TPU:1, one launch (start us, length us, event | category | flops | bytes accessed | tf_op | source)
XLA Modules:
  0.0 42.2 jit_solution(16805316910948392389)
XLA Ops:
  0.0 39.9 %shard_map.73 = f32[16,16,8,128]{3,2,1,0:T(8,128)} custom-call(f32[3,136]{1,0:T(4,128)} %constant.4.clone.rows, f32[8,128]{1,0:T(8,128)} %constant.5.clone.levels, f32[16,16,8,128]{3,2,1,0:T(8,128)} %bitcast.10, s32[2,12]{1,0:T(2,128)} %bitcast.13, f32[12,1,16]{2,1,0:T(1,128)} %bitcast.12, f32[1,12]{1,0:T(1,128)} %angle_hbm.1, s32[2,1536]{1,0:T(2,128)} %bitcast.11), custom_call_target="tpu_custom_call" | custom-call | tf_op jit(solution)/shard_map/pallas_call | solution.py:768
  39.9 2.3 %copy.9 = f32[1,16,16,8,128]{4,3,2,1,0:T(8,128)} copy(f32[1,16,16,8,128]{4,3,2,1,0:T(8,128)} %bitcast.9) | data formatting | bytes 2097152
